TPU v7x, 32 devices: a whole 2x2x4 slice. The times are simulated.
32 devices in a mesh: tgt: 16 (over z, y, core), sup: 2 (over x).
Axes of the slice: x: 2, y: 2, z: 4, core: 2. Of those that a mesh axis runs over, the one named last changes fastest.
Arguments:
- targets: float32 [128, 3, 1024], P('tgt'), may hold values from -4 to 4
- labels: int32 [128], P('tgt'), may hold values from 0 to 99
- support_slots: float32 [16, 64, 3, 1024], P('tgt', 'sup'), may hold values from -4 to 4
- block_owner: int32 [4], replicated, may hold values from 0 to 15, as said below
- dual_coeffs: float32 [4, 64, 100], P(None, 'sup'), may hold values from -0.15 to 0.15
Outputs:
- predictions: float32 [128, 100], P('tgt')
- support_grad: float32 [4, 64, 3, 1024], P(None, 'sup')
Inputs may be any that keep to these rules, and one draw needn't show every extreme that they name: 4 distinct slot indices, among them 0 and 15; block b is support_slots[block_owner[b]], and the other slots are never read.
All inputs are finite; a program needn't handle non-finite values.
Results may differ from a plain program's by a relative error of at most 0.0001.
Values sent between devices are 32-bit elements; how exact they have to be, the bound alone decides.
A program may use at most 128 MiB of HBM per device.

v0:
```python
import functools

import jax
import jax.numpy as jnp
from jax import lax
from jax.experimental import pallas as pl
from jax.experimental.pallas import tpu as pltpu
from jax.sharding import PartitionSpec as P

SIDE = 32
LANES = 128
CHUNK = 8
MESH = pl.DeviceIdType.MESH

weight_variance = 1.6
bias_variance = 0.1
loss_weight = 64.0
q = 2.0 / 3.141592653589793
w9 = weight_variance / 9.0

HALF = (
    0.9999998807907104, 0.16668881475925446, 0.07438822090625763,
    0.05069158226251602, 0.0044584982098147, 0.06837297230958939,
)
MIDDLE = (
    1.0000003576278687, 0.16661593317985535, 0.0763598307967186, 0.03124197944998741,
    0.09119893610477448, -0.11032058298587799, 0.1385442167520523,
)
LAST = (
    0.9999997615814209, 0.16670268774032593, 0.07408007979393005,
    0.0530407689511776, -0.0027404483407735825, 0.07600238919258118,
)


def polynomial(x, coefficients):
    total = jnp.full_like(x, coefficients[-1])
    for value in coefficients[-2::-1]:
        total = total * x + value
    return total


def wide_arcsin(z, complement, r):
    cosine = complement * r
    half = z * lax.rsqrt(2.0 + 2.0 * cosine)
    return (half + half) * polynomial(0.5 - 0.5 * cosine, HALF)


def stage_sizes(devices):
    bits = devices.bit_length() - 1
    low = max((bits - 1) // 2, 0)
    return [size for size in (min(devices, 2), 2 ** low, 2 ** (bits - 1 - low)) if size > 1]


class Stages:
    def __init__(self, sizes):
        self.sizes = sizes
        self.me = lax.axis_index("tgt")
        self.strides, self.digits = [], []
        stride = 1
        for size in sizes:
            self.strides.append(stride)
            self.digits.append(lax.rem(self.me // stride, size))
            stride = stride * size

    def place(self, device):
        total = 0
        for size, stride in zip(self.sizes, self.strides):
            total = total * size + lax.rem(device // stride, size)
        return total

    def peer(self, stage, step):
        digit = lax.rem(self.digits[stage] + step, self.sizes[stage])
        return digit, self.me + (digit - self.digits[stage]) * self.strides[stage]

    def base(self, stage, rows):
        total = 0
        for size, digit in zip(self.sizes[:stage + 1], self.digits):
            rows = rows // size
            total = total + digit * rows
        return total

    def back_copies(self, out_ref, piece, first, rows, stage, send, receive):
        held = rows
        for size in self.sizes[:stage + 1]:
            held = held // size
        place = pl.ds(pl.multiple_of(first + self.base(stage, rows), 8), held)
        before = sum(size - 1 for size in self.sizes[:stage])
        copies = []
        for step in range(1, self.sizes[stage]):
            copies.append(pltpu.make_async_remote_copy(
                src_ref=out_ref.at[place],
                dst_ref=out_ref.at[place],
                send_sem=send.at[piece, before + step - 1],
                recv_sem=receive.at[piece, before + step - 1],
                device_id={"tgt": self.peer(stage, step)[1]},
                device_id_type=MESH,
            ))
        return copies


def start_all(copies):
    for copy in copies:
        copy.start()
    return copies


def all_reduce_body(sizes, pieces, x_ref, out_ref, *scratch):
    stages = len(sizes)
    received = scratch[:stages]
    partial = scratch[stages:2 * stages - 1]
    send_sem, recv_sem, send_back, recv_back = scratch[2 * stages - 1:]
    where = Stages(sizes)
    barrier = pltpu.get_barrier_semaphore()
    for stage, size in enumerate(sizes):
        for step in range(1, size):
            pl.semaphore_signal(
                barrier, inc=1, device_id={"tgt": where.peer(stage, step)[1]},
                device_id_type=MESH,
            )
    pl.semaphore_wait(barrier, sum(size - 1 for size in sizes))
    rows = x_ref.shape[0] // pieces
    held = [rows]
    for size in sizes:
        held.append(held[-1] // size)

    def source(stage, piece):
        if stage == 0:
            return x_ref.at[pl.ds(piece * rows, rows)]
        return partial[stage - 1].at[piece]

    def send(stage, piece):
        size = sizes[stage]
        before = sum(other - 1 for other in sizes[:stage])
        copies = []
        for step in range(1, size):
            digit, device = where.peer(stage, step)
            part = pl.ds(pl.multiple_of(digit * held[stage + 1], 8), held[stage + 1])
            copies.append(pltpu.make_async_remote_copy(
                src_ref=source(stage, piece).at[part],
                dst_ref=received[stage].at[piece, step - 1],
                send_sem=send_sem.at[piece, before + step - 1],
                recv_sem=recv_sem.at[piece, before + step - 1],
                device_id={"tgt": device},
                device_id_type=MESH,
            ))
        return start_all(copies)

    def add(stage, piece, copies):
        part = pl.ds(
            pl.multiple_of(where.digits[stage] * held[stage + 1], 8), held[stage + 1]
        )
        total = source(stage, piece)[part]
        for copy in copies:
            copy.wait()
        for slot in range(sizes[stage] - 1):
            total = total + received[stage][piece, slot]
        if stage + 1 < stages:
            partial[stage][piece] = total
        else:
            place = pl.multiple_of(piece * rows + where.base(stage, rows), 8)
            out_ref[pl.ds(place, held[stage + 1])] = total

    def back(step, piece):
        return start_all(where.back_copies(
            out_ref, piece, piece * rows, rows, stages - 1 - step, send_back, recv_back
        ))

    pending = [send(0, piece) for piece in range(pieces)]
    for tick in range(pieces + 2 * stages - 1):
        for piece in range(pieces):
            level = tick - piece
            if level < 0 or level >= 2 * stages:
                continue
            if level < stages:
                add(level, piece, pending[piece])
            else:
                for copy in pending[piece]:
                    copy.wait()
            if level + 1 < stages:
                pending[piece] = send(level + 1, piece)
            elif level + 1 < 2 * stages:
                pending[piece] = back(level + 1 - stages, piece)


def all_reduce(x, devices, collective_id):
    sizes = stage_sizes(devices)
    pieces = max(k for k in (1, 2, 3) if x.shape[0] % (k * devices * 8) == 0)
    rows = x.shape[0] // pieces
    received, partial = [], []
    for size in sizes:
        rows = rows // size
        received.append(pltpu.VMEM((pieces, size - 1, rows, LANES), jnp.float32))
        partial.append(pltpu.VMEM((pieces, rows, LANES), jnp.float32))
    copies = sum(size - 1 for size in sizes)
    return pl.pallas_call(
        functools.partial(all_reduce_body, sizes, pieces),
        out_shape=jax.ShapeDtypeStruct(x.shape, x.dtype),
        in_specs=[pl.BlockSpec(memory_space=pltpu.VMEM)],
        out_specs=pl.BlockSpec(memory_space=pltpu.VMEM),
        scratch_shapes=received + partial[:-1] + [pltpu.SemaphoreType.DMA((pieces, copies))] * 4,
        compiler_params=pltpu.CompilerParams(
            collective_id=collective_id, has_side_effects=True, vmem_limit_bytes=24 << 20
        ),
        name="sum_over_targets",
    )(x)


def gather_body(devices, channels, blocks, owner_ref, x_ref, out_ref, *scratch):
    slots = scratch[:channels]
    send_sem, recv_sem, send_back, recv_back = scratch[channels:]
    sizes = stage_sizes(devices)
    stages = len(sizes)
    where = Stages(sizes)
    me = where.me
    barrier = pltpu.get_barrier_semaphore()
    for step in range(1, devices):
        pl.semaphore_signal(
            barrier, inc=1, device_id={"tgt": lax.rem(me + step, devices)}, device_id_type=MESH
        )
    pl.semaphore_wait(barrier, devices - 1)
    packed = x_ref.shape[1] // channels
    copies = []
    for c in range(channels):
        part = pl.ds(c * packed, packed)
        copies.append([])
        for step in range(1, devices):
            device = lax.rem(me + step, devices)
            copies[c].append(pltpu.make_async_remote_copy(
                src_ref=x_ref.at[where.place(device), part],
                dst_ref=slots[c].at[me],
                send_sem=send_sem.at[c, step - 1],
                recv_sem=recv_sem.at[c, step - 1],
                device_id={"tgt": device},
                device_id_type=MESH,
            ))
        start_all(copies[c])
    for c in range(channels):
        slots[c][me] = x_ref[where.place(me), pl.ds(c * packed, packed)]
    rows = out_ref.shape[0] // channels
    chunk = rows // devices
    groups = chunk // packed
    width = LANES // groups
    block = lax.broadcasted_iota(jnp.int32, (packed, LANES), 1) // width
    base = where.base(stages - 1, rows)
    pending = []
    for c in range(channels):
        for copy in copies[c]:
            copy.wait()
        parts = [slots[c][owner_ref[b]] for b in range(blocks)]
        for k in range(groups):
            total = jnp.zeros((packed, LANES), jnp.float32)
            for b in range(blocks):
                shift = (width * (b - k)) % LANES
                moved = pltpu.roll(parts[b], shift, 1) if shift else parts[b]
                total = jnp.where(block == b, moved, total)
            out_ref[pl.ds(pl.multiple_of(c * rows + base + k * packed, 8), packed)] = total
        pending.append(start_all(where.back_copies(
            out_ref, c, c * rows, rows, stages - 1, send_back, recv_back
        )))
    for tick in range(channels + stages - 1):
        for c in range(channels):
            level = tick - c
            if level < 0 or level >= stages:
                continue
            for copy in pending[c]:
                copy.wait()
            if level + 1 < stages:
                pending[c] = start_all(where.back_copies(
                    out_ref, c, c * rows, rows, stages - 2 - level, send_back, recv_back
                ))


def gather(slot, owner, devices):
    per_block, channels, pixels = slot.shape
    blocks = owner.shape[0]
    groups = LANES // per_block
    packed = pixels // devices // groups
    x = slot.reshape(per_block, channels, devices, groups, packed)
    x = jnp.transpose(x, (2, 1, 4, 3, 0)).reshape(devices, channels * packed, LANES)
    copies = sum(size - 1 for size in stage_sizes(devices))
    vmem = pl.BlockSpec(memory_space=pltpu.VMEM)
    return pl.pallas_call(
        functools.partial(gather_body, devices, channels, blocks),
        out_shape=jax.ShapeDtypeStruct((channels * pixels, LANES), jnp.float32),
        in_specs=[pl.BlockSpec(memory_space=pltpu.SMEM), vmem],
        out_specs=vmem,
        scratch_shapes=[pltpu.VMEM((devices, packed, LANES), jnp.float32)] * channels + [
            pltpu.SemaphoreType.DMA((channels, devices - 1)),
            pltpu.SemaphoreType.DMA((channels, devices - 1)),
            pltpu.SemaphoreType.DMA((channels, copies)),
            pltpu.SemaphoreType.DMA((channels, copies)),
        ],
        compiler_params=pltpu.CompilerParams(
            collective_id=0, has_side_effects=True, vmem_limit_bytes=24 << 20
        ),
        name="gather_supports",
    )(owner, x)


def tangent_body(
    n_sup, channels, s_ref, raw_ref, label_ref, dual_ref, pred_ref, grad_ref,
    f1, f2, f3, f4, z1_ref, r1_ref, z2_ref, r2_ref, th2_ref, n3_ref, t_ref, u_ref, sb_ref, vb_ref, sf_ref, nb_ref, sum_ref, part_ref,
    arrived, send_sem, recv_sem,
):
    pixels = SIDE * SIDE
    me = lax.axis_index("sup")
    barrier = pltpu.get_barrier_semaphore()
    for step in range(1, n_sup):
        pl.semaphore_signal(
            barrier, inc=1, device_id={"sup": lax.rem(me + step, n_sup)}, device_id_type=MESH
        )

    lane = lax.broadcasted_iota(jnp.int32, (8, LANES), 1)
    t_ref[...] = jnp.zeros(t_ref.shape, jnp.float32)
    for c in range(channels):
        image = raw_ref[:, c, :]
        for row in range(SIDE):
            t_ref[c, row, :, :SIDE] = image[:, row * SIDE:(row + 1) * SIDE]

    def lane_box(x):
        none = jnp.zeros((1, 8, LANES), jnp.float32)
        total = x + jnp.concatenate([none, x[:-1]]) + jnp.concatenate([x[1:], none])
        left = jnp.where(lane == 0, 0.0, pltpu.roll(total, 1, 2))
        right = jnp.where(lane == SIDE - 1, 0.0, pltpu.roll(total, LANES - 1, 2))
        return total + left + right

    power = t_ref[0] * t_ref[0]
    for c in range(1, channels):
        power = power + t_ref[c] * t_ref[c]
    n_t = (w9 / channels) * lane_box(power) + bias_variance
    for layer in range(3):
        b_t = 1.0 + 2.0 * n_t
        u_ref[layer] = lax.rsqrt(b_t)
        if layer < 2:
            z_t = 2.0 * n_t / b_t
            if layer == 0:
                rest = 1.0 - z_t * z_t
                angle_t = wide_arcsin(z_t, rest, lax.rsqrt(rest))
            else:
                angle_t = z_t * polynomial(z_t * z_t, MIDDLE)
            angle_t = jnp.where(lane < SIDE, angle_t, 0.0)
            n_t = (w9 * q) * lane_box(angle_t) + bias_variance

    for field in (f1, f2, f3, f4):
        for row in (0, SIDE + 1):
            field[row] = jnp.zeros(field.shape[1:], jnp.float32)

        def border(row, carry, field=field):
            for column in (0, SIDE + 1):
                field[row, column] = jnp.zeros(field.shape[2:], jnp.float32)
            return carry

        lax.fori_loop(1, SIDE + 1, border, 0)

    zero_row = jnp.zeros((SIDE, LANES), jnp.float32)
    for slot in range(2):
        sf_ref[slot, pl.ds(0, SIDE)] = zero_row
        sf_ref[slot, pl.ds(SIDE + pixels, SIDE)] = zero_row
    column = lax.broadcasted_iota(jnp.int32, (SIDE, LANES), 0)

    def line(row):
        return pl.ds(pl.multiple_of(row * SIDE, SIDE), SIDE)

    def flat_box(slot, row):
        x = (
            sf_ref[slot, line(row)] + sf_ref[slot, line(row + 1)] + sf_ref[slot, line(row + 2)]
        )
        left = jnp.where(column == 0, 0.0, pltpu.roll(x, 1, 0))
        right = jnp.where(column == SIDE - 1, 0.0, pltpu.roll(x, SIDE - 1, 0))
        return x + left + right

    def squares(row, carry):
        total = jnp.zeros((SIDE, LANES), jnp.float32)
        for c in range(channels):
            image = s_ref[c, line(row)]
            total = total + image * image
            for j in range(SIDE):
                sb_ref[c, row * SIDE + j] = image[j:j + 1]
        sf_ref[0, line(row + 1)] = total
        return carry

    lax.fori_loop(0, SIDE, squares, 0)

    def own_layer(layer):
        source, target = layer % 2, (layer + 1) % 2
        scale = w9 / channels if layer == 0 else w9 * q

        def body(row, carry):
            n = scale * flat_box(source, row) + bias_variance
            b = 1.0 + 2.0 * n
            v = lax.rsqrt(b)
            nb_ref[layer, line(row)] = n
            for j in range(SIDE):
                vb_ref[layer, row * SIDE + j] = v[j:j + 1]
            if layer < 2:
                z = 2.0 * n / b
                if layer == 0:
                    complement = 1.0 - z * z
                    angle = wide_arcsin(z, complement, lax.rsqrt(complement))
                else:
                    angle = z * polynomial(z * z, MIDDLE)
                sf_ref[target, line(row + 1)] = angle
            return carry

        lax.fori_loop(0, SIDE, body, 0)

    for layer in range(3):
        own_layer(layer)

    coeffs = dual_ref[...].reshape(-1, dual_ref.shape[2])
    if coeffs.shape[0] < LANES:
        coeffs = jnp.pad(coeffs, ((0, LANES - coeffs.shape[0]), (0, 0)))

    def rows(function, init=0):
        def four(step, carry):
            return function(step * 4 + 2, function(step * 4, carry))

        return lax.fori_loop(0, SIDE // 4, four, init)

    def spread(ref, k, row, c0):
        values = ref[k, row]
        return jnp.stack(
            [jnp.broadcast_to(values[:, c0 + j:c0 + j + 1], (8, LANES)) for j in range(CHUNK)]
        )

    def across(ref, k, row, c0):
        values = ref[k, pl.ds(row * SIDE + c0, CHUNK)]
        return jnp.broadcast_to(values, (CHUNK, 8, LANES))

    def box(ref, row, c0):
        lines = [ref[row + k, pl.ds(c0, CHUNK + 2)] for k in range(4)]
        middle = lines[1] + lines[2]
        sums = [lines[0] + middle, middle + lines[3]]
        return [x[:-2] + x[1:-1] + x[2:] for x in sums]

    def put(ref, row, c0, value):
        ref[row + 1, pl.ds(c0 + 1, CHUNK)] = value

    def keep(ref, row, c0, value):
        ref[row, pl.ds(c0, CHUNK)] = value

    def kept(ref, row, c0):
        return ref[row, pl.ds(c0, CHUNK)]

    starts = range(0, SIDE, CHUNK)

    def pass_cross(first, carry):
        for row in (first, first + 1):
            for c0 in starts:
                total = spread(t_ref, 0, row, c0) * across(sb_ref, 0, row, c0)
                for c in range(1, channels):
                    total = total + spread(t_ref, c, row, c0) * across(sb_ref, c, row, c0)
                put(f1, row, c0, total)
        return carry

    def pass_first(first, carry):
        for c0 in starts:
            for row, value in zip((first, first + 1), box(f1, first, c0)):
                uv = spread(u_ref, 0, row, c0) * across(vb_ref, 0, row, c0)
                z = uv * ((2.0 * w9 / channels) * value + 2.0 * bias_variance)
                complement = 1.0 - z * z
                r = lax.rsqrt(complement)
                keep(z1_ref, row, c0, z)
                keep(r1_ref, row, c0, r)
                put(f2, row, c0, wide_arcsin(z, complement, r))
                put(f3, row, c0, z * r)
        return carry

    def pass_second(first, carry):
        for c0 in starts:
            pairs = zip((first, first + 1), box(f2, first, c0), box(f3, first, c0))
            for row, angles, tangents in pairs:
                uv = spread(u_ref, 1, row, c0) * across(vb_ref, 1, row, c0)
                z = uv * ((2.0 * w9 * q) * angles + 2.0 * bias_variance)
                tangent = z + uv * ((2.0 * w9 * q) * tangents)
                square = z * z
                r = lax.rsqrt(1.0 - square)
                keep(z2_ref, row, c0, z)
                keep(r2_ref, row, c0, r)
                keep(th2_ref, row, c0, tangent)
                put(f1, row, c0, z * polynomial(square, MIDDLE))
                put(f4, row, c0, tangent * r)
        return carry

    def pass_third(first, carry):
        for c0 in starts:
            pairs = zip((first, first + 1), box(f1, first, c0), box(f4, first, c0))
            for row, angles, tangents in pairs:
                uv = spread(u_ref, 2, row, c0) * across(vb_ref, 2, row, c0)
                z = uv * ((2.0 * w9 * q) * angles + 2.0 * bias_variance)
                tangent = z + uv * ((2.0 * w9 * q) * tangents)
                square = z * z
                r = lax.rsqrt(1.0 - square)
                carry = carry + jnp.sum(z * polynomial(square, LAST) + tangent * r, axis=0)
                slope = (2.0 * q * w9) * (uv * r)
                bent = tangent * (r * r)
                put(f3, row, c0, slope)
                put(f2, row, c0, slope * (2.0 + z * bent))
                keep(n3_ref, row, c0, r * (z + bent))
        return carry

    rows(pass_cross)
    rows(pass_first)
    rows(pass_second)
    mean = rows(pass_third, jnp.zeros((8, LANES), jnp.float32))
    kernel = (weight_variance * q / pixels) * mean + bias_variance

    part_ref[...] = jnp.dot(
        kernel, coeffs, precision=lax.Precision.HIGHEST,
        preferred_element_type=jnp.float32,
    )
    pl.semaphore_wait(barrier, n_sup - 1)
    copies = []
    for step in range(1, n_sup):
        copy = pltpu.make_async_remote_copy(
            src_ref=part_ref,
            dst_ref=arrived.at[step - 1],
            send_sem=send_sem.at[step - 1],
            recv_sem=recv_sem.at[step - 1],
            device_id={"sup": lax.rem(me + step, n_sup)},
            device_id_type=MESH,
        )
        copy.start()
        copies.append(copy)
    for copy in copies:
        copy.wait()
    predictions = part_ref[...]
    for step in range(n_sup - 1):
        predictions = predictions + arrived[step]
    pred_ref[...] = predictions
    target = lax.broadcasted_iota(jnp.int32, predictions.shape, 0)
    label = jnp.zeros(predictions.shape, jnp.int32)
    for k in range(8):
        label = jnp.where(target == k, label_ref[k], label)
    onehot = (label == lax.broadcasted_iota(jnp.int32, predictions.shape, 1)).astype(jnp.float32)
    error = loss_weight * (predictions - onehot)
    weights = lax.dot_general(
        error, coeffs, (((1,), (1,)), ((), ())), precision=lax.Precision.HIGHEST,
        preferred_element_type=jnp.float32,
    )
    kappa = (weight_variance / pixels) * weights

    sublane = lax.broadcasted_iota(jnp.int32, (8, LANES), 0)
    odd = [lax.rem(sublane // step, 2) == 1 for step in (1, 2, 4)]

    def total_rows(value):
        items = [value[j] for j in range(CHUNK)]
        for step, mask in zip((1, 2, 4), odd):
            items = [
                jnp.where(mask, second, first)
                + pltpu.roll(jnp.where(mask, first, second), step, 0)
                for first, second in zip(items[::2], items[1::2])
            ]
        return items[0]

    def pass_back_second(first, carry):
        for c0 in starts:
            pairs = zip((first, first + 1), box(f2, first, c0), box(f3, first, c0))
            for row, up, mean_up in pairs:
                uv = spread(u_ref, 1, row, c0) * across(vb_ref, 1, row, c0)
                z = kept(z2_ref, row, c0)
                r = kept(r2_ref, row, c0)
                up = kappa * up
                mean_up = kappa * mean_up
                bent = mean_up * kept(th2_ref, row, c0) * (r * r)
                slope = (2.0 * q * w9) * (uv * r)
                put(f4, row, c0, mean_up * slope)
                put(f1, row, c0, slope * (up + mean_up + bent * z))
                place = pl.ds(pl.multiple_of(row * SIDE + c0, CHUNK), CHUNK)
                nb_ref[4, place] = total_rows(r * (up * z + bent))
                nb_ref[5, place] = total_rows(kappa * kept(n3_ref, row, c0))
        return carry

    def pass_back_first(first, carry):
        for c0 in starts:
            pairs = zip((first, first + 1), box(f1, first, c0), box(f4, first, c0))
            for row, up, mean_up in pairs:
                uv = spread(u_ref, 0, row, c0) * across(vb_ref, 0, row, c0)
                r = kept(r1_ref, row, c0)
                joined = r * (up + (r * r) * mean_up)
                put(f2, row, c0, (2.0 * q * w9 / channels) * (uv * joined))
                place = pl.ds(pl.multiple_of(row * SIDE + c0, CHUNK), CHUNK)
                nb_ref[3, place] = total_rows(kept(z1_ref, row, c0) * joined)
        return carry

    rows(pass_back_second)
    rows(pass_back_first)

    def own_back(layer):
        source, target = (layer + 1) % 2, layer % 2

        def body(row, carry):
            n = nb_ref[layer, line(row)]
            b = 1.0 + 2.0 * n
            value = nb_ref[3 + layer, line(row)] * (-q / b)
            if layer < 2:
                value = value + (2.0 * w9 * q) * flat_box(source, row) * (
                    lax.rsqrt(1.0 + 4.0 * n) / b
                )
            sf_ref[target, line(row + 1)] = value
            return carry

        lax.fori_loop(0, SIDE, body, 0)

    for layer in (2, 1, 0):
        own_back(layer)

    def pass_images(first, carry):
        for row in (first, first + 1):
            own = (2.0 * w9 / channels) * flat_box(0, row)
            for c in range(channels):
                sum_ref[c, line(row)] = own * s_ref[c, line(row)]
        for c0 in starts:
            for row, value in zip((first, first + 1), box(f2, first, c0)):
                place = pl.ds(pl.multiple_of(row * SIDE + c0, CHUNK), CHUNK)
                for c in range(channels):
                    sum_ref[c, place] += total_rows(value * spread(t_ref, c, row, c0))
        return carry

    rows(pass_images)
    for c in range(channels):
        def turn(group, carry, c=c):
            place = pl.ds(pl.multiple_of(group * LANES, LANES), LANES)
            grad_ref[c * (pixels // LANES) + group] = jnp.transpose(sum_ref[c, place])
            return carry

        lax.fori_loop(0, pixels // LANES, turn, 0)


def tangent(s, targets, labels, dual_coeffs, n_sup):
    channels = s.shape[0]
    pixels = SIDE * SIDE
    classes = dual_coeffs.shape[2]
    field = pltpu.VMEM((SIDE + 2, SIDE + 2, 8, LANES), jnp.float32)
    plain = pltpu.VMEM((SIDE, SIDE, 8, LANES), jnp.float32)
    vmem = pl.BlockSpec(memory_space=pltpu.VMEM)
    return pl.pallas_call(
        functools.partial(tangent_body, n_sup, channels),
        out_shape=(
            jax.ShapeDtypeStruct((8, classes), jnp.float32),
            jax.ShapeDtypeStruct((channels * pixels // LANES, LANES, LANES), jnp.float32),
        ),
        in_specs=[vmem, vmem, pl.BlockSpec(memory_space=pltpu.SMEM), vmem],
        out_specs=(vmem, vmem),
        scratch_shapes=[field] * 4 + [plain] * 6 + [
            pltpu.VMEM((channels, SIDE, 8, LANES), jnp.float32),
            pltpu.VMEM((3, SIDE, 8, LANES), jnp.float32),
            pltpu.VMEM((channels, pixels, 1, LANES), jnp.float32),
            pltpu.VMEM((3, pixels, 1, LANES), jnp.float32),
            pltpu.VMEM((2, pixels + 2 * SIDE, LANES), jnp.float32),
            pltpu.VMEM((6, pixels, LANES), jnp.float32),
            pltpu.VMEM((channels, pixels, LANES), jnp.float32),
            pltpu.VMEM((8, classes), jnp.float32),
            pltpu.VMEM((n_sup - 1, 8, classes), jnp.float32),
            pltpu.SemaphoreType.DMA((n_sup - 1,)),
            pltpu.SemaphoreType.DMA((n_sup - 1,)),
        ],
        compiler_params=pltpu.CompilerParams(
            collective_id=1, has_side_effects=True, vmem_limit_bytes=60 << 20
        ),
        name="tangent_kernel",
    )(s, targets, labels, dual_coeffs)


def local(n_tgt, n_sup, targets, labels, support_slots, block_owner, dual_coeffs):
    blocks, per_block, _ = dual_coeffs.shape
    channels = targets.shape[1]
    pixels = targets.shape[2]
    supports = blocks * per_block
    if supports == LANES and (pixels * per_block) % (n_tgt * LANES * 8) == 0:
        s = gather(support_slots[0], block_owner, n_tgt)
    else:
        mine = block_owner == lax.axis_index("tgt")
        slot = jnp.transpose(support_slots[0], (1, 2, 0))
        own = jnp.where(mine[None, None, :, None], slot[:, :, None, :], 0.0)
        own = own.reshape(channels * pixels, supports)
        s = all_reduce(jnp.pad(own, ((0, 0), (0, LANES - supports))), n_tgt, 0)
    s = s.reshape(channels, pixels, LANES)

    predictions, grad = tangent(s, targets, labels, dual_coeffs, n_sup)
    grad = all_reduce(grad.reshape(channels * pixels, LANES), n_tgt, 2)
    grad = grad.reshape(channels, pixels // LANES, LANES, LANES)[:, :, :supports]
    grad = jnp.transpose(grad, (2, 0, 1, 3)).reshape(blocks, per_block, channels, pixels)
    return predictions, grad


def solution(mesh):
    return jax.shard_map(
        functools.partial(local, mesh.shape["tgt"], mesh.shape["sup"]),
        mesh=mesh,
        in_specs=(
            P("tgt", None, None),
            P("tgt"),
            P("tgt", "sup", None, None),
            P(),
            P(None, "sup", None),
        ),
        out_specs=(P("tgt", None), P(None, "sup", None, None)),
        check_vma=False,
    )
```

profile of v0, /device:TPU:0, one launch (start us, length us, event | category | flops | bytes accessed | tf_op | source)
XLA Modules:
  0.0 136.4 jit_solution(12955593154274847423)
XLA Ops:
  0.6 1.6 %copy.11.raw_ref = f32[8,3,1024]{2,1,0:T(4,128)} copy(f32[8,3,1024]{2,0,1:T(8,128)} %param.5) | data formatting | bytes 196608 | tf_op args[0]
  2.2 1.5 %copy.9 = f32[1,32,3,1024]{1,3,2,0:T(8,128)S(1)} copy(f32[1,32,3,1024]{3,1,2,0:T(8,128)} %param.7) | data formatting | bytes 786432 | tf_op args[2]
  3.7 0.7 copy.10
  4.4 0.0 copy-start.2
  4.4 0.7 reshape.19.x_ref
  5.1 0.0 copy-done.2
  5.1 34.4 %gather_supports.1 = f32[3072,128]{1,0:T(8,128)S(1)} custom-call(s32[4]{0:T(128)S(1)} %copy-done.2, f32[16,48,128]{2,1,0:T(8,128)S(1)} %reshape.19.x_ref), custom_call_target="tpu_custom_call" | custom-call | tf_op jit(solution)/shard_map/gather_supports/pallas_call | solution.py:282
  39.5 0.0 copy-start
  39.5 1.1 copy-done
  40.7 51.3 %tangent_kernel.1 = (f32[8,100]{1,0:T(8,128)}, f32[24,128,128]{2,1,0:T(8,128)}) custom-call(f32[3,1024,128]{2,1,0:T(8,128)} %bitcast.14, f32[8,3,1024]{2,1,0:T(4,128)} %copy.11.raw_ref, s32[8]{0:T(128)} %label_ref.1, f32[4,32,100]{2,1,0:T(8,128)} %dual_ref.1), custom_call_target="tpu_custom_call" | custom-call | tf_op jit(solution)/shard_map/tangent_kernel/pallas_call | solution.py:637
  92.0 0.0 copy-start.1
  92.0 1.4 %copy-done.1 = f32[24,128,128]{2,1,0:T(8,128)S(1)} copy-done((f32[24,128,128]{2,1,0:T(8,128)S(1)}, f32[24,128,128]{2,1,0:T(8,128)}, u32[]{:S(2)}) %copy-start.1) | copy-done | bytes 1572888
  93.4 39.9 %sum_over_targets.1 = f32[3072,128]{1,0:T(8,128)S(1)} custom-call(f32[3072,128]{1,0:T(8,128)S(1)} %bitcast.15), custom_call_target="tpu_custom_call" | custom-call | tf_op jit(solution)/shard_map/sum_over_targets/pallas_call | solution.py:195
  133.4 0.9 copy.15
  134.3 0.2 reshape.23
  134.5 0.0 copy-start.3
  134.5 1.2 copy.13
  135.8 0.0 copy-done.3
  135.8 0.6 copy.17
Async XLA Ops:
  4.4 0.7 copy-start.2
  39.5 1.1 copy-start
  92.0 1.4 %copy-start.1 = (f32[24,128,128]{2,1,0:T(8,128)S(1)}, f32[24,128,128]{2,1,0:T(8,128)}, u32[]{:S(2)}) copy-start(f32[24,128,128]{2,1,0:T(8,128)} %get-tuple-element.5) | copy-start | bytes 4718596
  134.5 1.3 copy-start.3
where the time goes:
time: 137 us; the launch traced here: 136 us
  Pallas kernels  126 us (92%)
  local copies, waits for them, and re-layouts  9.97 us (7%)
    pallas_call x1, Pallas kernels, tangent(): pl.pallas_call(functools.partial(tangent_body, n_sup, channels), out_shap...  51.3 us
    pallas_call x1, Pallas kernels, all_reduce(): pl.pallas_call(functools.partial(all_reduce_body, sizes, pieces), out_sha...  39.9 us
    pallas_call x1, Pallas kernels, gather(): pl.pallas_call(functools.partial(gather_body, devices, channels, blocks),...  34.4 us
    unnamed x12, local copies, waits for them, and re-layouts  7.46 us

commit v1 on v0

--- a/solution.py
+++ b/solution.py
@@ -104,20 +104,21 @@
     return copies
 
 
-def all_reduce_body(sizes, pieces, x_ref, out_ref, *scratch):
+def all_reduce_body(sizes, pieces, greet, x_ref, out_ref, *scratch):
     stages = len(sizes)
     received = scratch[:stages]
     partial = scratch[stages:2 * stages - 1]
     send_sem, recv_sem, send_back, recv_back = scratch[2 * stages - 1:]
     where = Stages(sizes)
-    barrier = pltpu.get_barrier_semaphore()
-    for stage, size in enumerate(sizes):
-        for step in range(1, size):
-            pl.semaphore_signal(
-                barrier, inc=1, device_id={"tgt": where.peer(stage, step)[1]},
-                device_id_type=MESH,
-            )
-    pl.semaphore_wait(barrier, sum(size - 1 for size in sizes))
+    if greet:
+        barrier = pltpu.get_barrier_semaphore()
+        for stage, size in enumerate(sizes):
+            for step in range(1, size):
+                pl.semaphore_signal(
+                    barrier, inc=1, device_id={"tgt": where.peer(stage, step)[1]},
+                    device_id_type=MESH,
+                )
+        pl.semaphore_wait(barrier, sum(size - 1 for size in sizes))
     rows = x_ref.shape[0] // pieces
     held = [rows]
     for size in sizes:
@@ -182,22 +183,28 @@
                 pending[piece] = back(level + 1 - stages, piece)
 
 
-def all_reduce(x, devices, collective_id):
+def all_reduce_scratch(rows, devices):
     sizes = stage_sizes(devices)
-    pieces = max(k for k in (1, 2, 3) if x.shape[0] % (k * devices * 8) == 0)
-    rows = x.shape[0] // pieces
+    pieces = max(k for k in (1, 2, 3) if rows % (k * devices * 8) == 0)
+    rows = rows // pieces
     received, partial = [], []
     for size in sizes:
         rows = rows // size
         received.append(pltpu.VMEM((pieces, size - 1, rows, LANES), jnp.float32))
         partial.append(pltpu.VMEM((pieces, rows, LANES), jnp.float32))
     copies = sum(size - 1 for size in sizes)
+    semaphores = [pltpu.SemaphoreType.DMA((pieces, copies))] * 4
+    return sizes, pieces, received + partial[:-1] + semaphores
+
+
+def all_reduce(x, devices, collective_id):
+    sizes, pieces, scratch = all_reduce_scratch(x.shape[0], devices)
     return pl.pallas_call(
-        functools.partial(all_reduce_body, sizes, pieces),
+        functools.partial(all_reduce_body, sizes, pieces, True),
         out_shape=jax.ShapeDtypeStruct(x.shape, x.dtype),
         in_specs=[pl.BlockSpec(memory_space=pltpu.VMEM)],
         out_specs=pl.BlockSpec(memory_space=pltpu.VMEM),
-        scratch_shapes=received + partial[:-1] + [pltpu.SemaphoreType.DMA((pieces, copies))] * 4,
+        scratch_shapes=scratch,
         compiler_params=pltpu.CompilerParams(
             collective_id=collective_id, has_side_effects=True, vmem_limit_bytes=24 << 20
         ),
@@ -205,19 +212,13 @@
     )(x)
 
 
-def gather_body(devices, channels, blocks, owner_ref, x_ref, out_ref, *scratch):
+def gather_body(devices, channels, blocks, meanwhile, owner_ref, x_ref, out_ref, *scratch):
     slots = scratch[:channels]
     send_sem, recv_sem, send_back, recv_back = scratch[channels:]
     sizes = stage_sizes(devices)
     stages = len(sizes)
     where = Stages(sizes)
     me = where.me
-    barrier = pltpu.get_barrier_semaphore()
-    for step in range(1, devices):
-        pl.semaphore_signal(
-            barrier, inc=1, device_id={"tgt": lax.rem(me + step, devices)}, device_id_type=MESH
-        )
-    pl.semaphore_wait(barrier, devices - 1)
     packed = x_ref.shape[1] // channels
     copies = []
     for c in range(channels):
@@ -236,6 +237,7 @@
         start_all(copies[c])
     for c in range(channels):
         slots[c][me] = x_ref[where.place(me), pl.ds(c * packed, packed)]
+    meanwhile()
     rows = out_ref.shape[0] // channels
     chunk = rows // devices
     groups = chunk // packed
@@ -270,87 +272,77 @@
                 ))
 
 
-def gather(slot, owner, devices):
+def pack_slot(slot, devices):
     per_block, channels, pixels = slot.shape
-    blocks = owner.shape[0]
     groups = LANES // per_block
     packed = pixels // devices // groups
     x = slot.reshape(per_block, channels, devices, groups, packed)
-    x = jnp.transpose(x, (2, 1, 4, 3, 0)).reshape(devices, channels * packed, LANES)
+    return jnp.transpose(x, (2, 1, 4, 3, 0)).reshape(devices, channels * packed, LANES)
+
+
+def gather_scratch(packed_shape, channels, devices):
+    _, rows, _ = packed_shape
     copies = sum(size - 1 for size in stage_sizes(devices))
-    vmem = pl.BlockSpec(memory_space=pltpu.VMEM)
-    return pl.pallas_call(
-        functools.partial(gather_body, devices, channels, blocks),
-        out_shape=jax.ShapeDtypeStruct((channels * pixels, LANES), jnp.float32),
-        in_specs=[pl.BlockSpec(memory_space=pltpu.SMEM), vmem],
-        out_specs=vmem,
-        scratch_shapes=[pltpu.VMEM((devices, packed, LANES), jnp.float32)] * channels + [
-            pltpu.SemaphoreType.DMA((channels, devices - 1)),
-            pltpu.SemaphoreType.DMA((channels, devices - 1)),
-            pltpu.SemaphoreType.DMA((channels, copies)),
-            pltpu.SemaphoreType.DMA((channels, copies)),
-        ],
-        compiler_params=pltpu.CompilerParams(
-            collective_id=0, has_side_effects=True, vmem_limit_bytes=24 << 20
-        ),
-        name="gather_supports",
-    )(owner, x)
+    return [pltpu.VMEM((devices, rows // channels, LANES), jnp.float32)] * channels + [
+        pltpu.SemaphoreType.DMA((channels, devices - 1)),
+        pltpu.SemaphoreType.DMA((channels, devices - 1)),
+        pltpu.SemaphoreType.DMA((channels, copies)),
+        pltpu.SemaphoreType.DMA((channels, copies)),
+    ]
 
 
 def tangent_body(
-    n_sup, channels, s_ref, raw_ref, label_ref, dual_ref, pred_ref, grad_ref,
-    f1, f2, f3, f4, z1_ref, r1_ref, z2_ref, r2_ref, th2_ref, n3_ref, t_ref, u_ref, sb_ref, vb_ref, sf_ref, nb_ref, sum_ref, part_ref,
-    arrived, send_sem, recv_sem,
+    bring, n_sup, channels, s_ref, raw_ref, label_ref, dual_ref, pred_ref, grad_ref,
+    f1, f2, f3, f4, z1_ref, r1_ref, z2_ref, r2_ref, th2_ref, n3_ref, t_ref, u_ref, sb_ref,
+    vb_ref, sf_ref, nb_ref, sum_ref, part_ref, arrived, send_sem, recv_sem,
 ):
     pixels = SIDE * SIDE
     me = lax.axis_index("sup")
-    barrier = pltpu.get_barrier_semaphore()
-    for step in range(1, n_sup):
-        pl.semaphore_signal(
-            barrier, inc=1, device_id={"sup": lax.rem(me + step, n_sup)}, device_id_type=MESH
-        )
-
-    lane = lax.broadcasted_iota(jnp.int32, (8, LANES), 1)
-    t_ref[...] = jnp.zeros(t_ref.shape, jnp.float32)
-    for c in range(channels):
-        image = raw_ref[:, c, :]
-        for row in range(SIDE):
-            t_ref[c, row, :, :SIDE] = image[:, row * SIDE:(row + 1) * SIDE]
-
-    def lane_box(x):
-        none = jnp.zeros((1, 8, LANES), jnp.float32)
-        total = x + jnp.concatenate([none, x[:-1]]) + jnp.concatenate([x[1:], none])
-        left = jnp.where(lane == 0, 0.0, pltpu.roll(total, 1, 2))
-        right = jnp.where(lane == SIDE - 1, 0.0, pltpu.roll(total, LANES - 1, 2))
-        return total + left + right
-
-    power = t_ref[0] * t_ref[0]
-    for c in range(1, channels):
-        power = power + t_ref[c] * t_ref[c]
-    n_t = (w9 / channels) * lane_box(power) + bias_variance
-    for layer in range(3):
-        b_t = 1.0 + 2.0 * n_t
-        u_ref[layer] = lax.rsqrt(b_t)
-        if layer < 2:
-            z_t = 2.0 * n_t / b_t
-            if layer == 0:
-                rest = 1.0 - z_t * z_t
-                angle_t = wide_arcsin(z_t, rest, lax.rsqrt(rest))
-            else:
-                angle_t = z_t * polynomial(z_t * z_t, MIDDLE)
-            angle_t = jnp.where(lane < SIDE, angle_t, 0.0)
-            n_t = (w9 * q) * lane_box(angle_t) + bias_variance
-
-    for field in (f1, f2, f3, f4):
-        for row in (0, SIDE + 1):
-            field[row] = jnp.zeros(field.shape[1:], jnp.float32)
-
-        def border(row, carry, field=field):
-            for column in (0, SIDE + 1):
-                field[row, column] = jnp.zeros(field.shape[2:], jnp.float32)
-            return carry
-
-        lax.fori_loop(1, SIDE + 1, border, 0)
+
+    def prepare():
+        lane = lax.broadcasted_iota(jnp.int32, (8, LANES), 1)
+        t_ref[...] = jnp.zeros(t_ref.shape, jnp.float32)
+        for c in range(channels):
+            image = raw_ref[:, c, :]
+            for row in range(SIDE):
+                t_ref[c, row, :, :SIDE] = image[:, row * SIDE:(row + 1) * SIDE]
+
+        def lane_box(x):
+            none = jnp.zeros((1, 8, LANES), jnp.float32)
+            total = x + jnp.concatenate([none, x[:-1]]) + jnp.concatenate([x[1:], none])
+            left = jnp.where(lane == 0, 0.0, pltpu.roll(total, 1, 2))
+            right = jnp.where(lane == SIDE - 1, 0.0, pltpu.roll(total, LANES - 1, 2))
+            return total + left + right
+
+        power = t_ref[0] * t_ref[0]
+        for c in range(1, channels):
+            power = power + t_ref[c] * t_ref[c]
+        n_t = (w9 / channels) * lane_box(power) + bias_variance
+        for layer in range(3):
+            b_t = 1.0 + 2.0 * n_t
+            u_ref[layer] = lax.rsqrt(b_t)
+            if layer < 2:
+                z_t = 2.0 * n_t / b_t
+                if layer == 0:
+                    rest = 1.0 - z_t * z_t
+                    angle_t = wide_arcsin(z_t, rest, lax.rsqrt(rest))
+                else:
+                    angle_t = z_t * polynomial(z_t * z_t, MIDDLE)
+                angle_t = jnp.where(lane < SIDE, angle_t, 0.0)
+                n_t = (w9 * q) * lane_box(angle_t) + bias_variance
+
+        for field in (f1, f2, f3, f4):
+            for row in (0, SIDE + 1):
+                field[row] = jnp.zeros(field.shape[1:], jnp.float32)
+
+            def border(row, carry, field=field):
+                for column in (0, SIDE + 1):
+                    field[row, column] = jnp.zeros(field.shape[2:], jnp.float32)
+                return carry
+
+            lax.fori_loop(1, SIDE + 1, border, 0)
+
+    bring(prepare)
 
     zero_row = jnp.zeros((SIDE, LANES), jnp.float32)
     for slot in range(2):
@@ -372,7 +364,7 @@
     def squares(row, carry):
         total = jnp.zeros((SIDE, LANES), jnp.float32)
         for c in range(channels):
-            image = s_ref[c, line(row)]
+            image = s_ref[pl.ds(pl.multiple_of(c * pixels + row * SIDE, SIDE), SIDE)]
             total = total + image * image
             for j in range(SIDE):
                 sb_ref[c, row * SIDE + j] = image[j:j + 1]
@@ -509,7 +501,6 @@
         kernel, coeffs, precision=lax.Precision.HIGHEST,
         preferred_element_type=jnp.float32,
     )
-    pl.semaphore_wait(barrier, n_sup - 1)
     copies = []
     for step in range(1, n_sup):
         copy = pltpu.make_async_remote_copy(
@@ -609,7 +600,7 @@
         for row in (first, first + 1):
             own = (2.0 * w9 / channels) * flat_box(0, row)
             for c in range(channels):
-                sum_ref[c, line(row)] = own * s_ref[c, line(row)]
+                sum_ref[c, line(row)] = own * s_ref[pl.ds(pl.multiple_of(c * pixels + row * SIDE, SIDE), SIDE)]
         for c0 in starts:
             for row, value in zip((first, first + 1), box(f2, first, c0)):
                 place = pl.ds(pl.multiple_of(row * SIDE + c0, CHUNK), CHUNK)
@@ -621,64 +612,105 @@
     for c in range(channels):
         def turn(group, carry, c=c):
             place = pl.ds(pl.multiple_of(group * LANES, LANES), LANES)
-            grad_ref[c * (pixels // LANES) + group] = jnp.transpose(sum_ref[c, place])
+            grad_ref[pl.ds(pl.multiple_of((c * (pixels // LANES) + group) * LANES, LANES), LANES)] = jnp.transpose(sum_ref[c, place])
             return carry
 
         lax.fori_loop(0, pixels // LANES, turn, 0)
 
 
-def tangent(s, targets, labels, dual_coeffs, n_sup):
-    channels = s.shape[0]
-    pixels = SIDE * SIDE
-    classes = dual_coeffs.shape[2]
-    field = pltpu.VMEM((SIDE + 2, SIDE + 2, 8, LANES), jnp.float32)
-    plain = pltpu.VMEM((SIDE, SIDE, 8, LANES), jnp.float32)
-    vmem = pl.BlockSpec(memory_space=pltpu.VMEM)
-    return pl.pallas_call(
-        functools.partial(tangent_body, n_sup, channels),
-        out_shape=(
-            jax.ShapeDtypeStruct((8, classes), jnp.float32),
-            jax.ShapeDtypeStruct((channels * pixels // LANES, LANES, LANES), jnp.float32),
-        ),
-        in_specs=[vmem, vmem, pl.BlockSpec(memory_space=pltpu.SMEM), vmem],
-        out_specs=(vmem, vmem),
-        scratch_shapes=[field] * 4 + [plain] * 6 + [
-            pltpu.VMEM((channels, SIDE, 8, LANES), jnp.float32),
-            pltpu.VMEM((3, SIDE, 8, LANES), jnp.float32),
-            pltpu.VMEM((channels, pixels, 1, LANES), jnp.float32),
-            pltpu.VMEM((3, pixels, 1, LANES), jnp.float32),
-            pltpu.VMEM((2, pixels + 2 * SIDE, LANES), jnp.float32),
-            pltpu.VMEM((6, pixels, LANES), jnp.float32),
-            pltpu.VMEM((channels, pixels, LANES), jnp.float32),
-            pltpu.VMEM((8, classes), jnp.float32),
-            pltpu.VMEM((n_sup - 1, 8, classes), jnp.float32),
-            pltpu.SemaphoreType.DMA((n_sup - 1,)),
-            pltpu.SemaphoreType.DMA((n_sup - 1,)),
-        ],
-        compiler_params=pltpu.CompilerParams(
-            collective_id=1, has_side_effects=True, vmem_limit_bytes=60 << 20
-        ),
-        name="tangent_kernel",
-    )(s, targets, labels, dual_coeffs)
+def program_body(n_tgt, n_sup, channels, blocks, gathered, counts, *refs):
+    refs = list(refs)
+
+    def take(count):
+        taken, refs[:count] = refs[:count], []
+        return taken
+
+    inputs = take(5 if gathered else 4)
+    pred_ref, out_ref = take(2)
+    grad_ref, = take(1)
+    support = take(1) if gathered else inputs[:1]
+    gather_refs = take(counts[0])
+    tangent_refs = take(counts[1])
+
+    barrier = pltpu.get_barrier_semaphore()
+    for axis, size in (("tgt", n_tgt), ("sup", n_sup)):
+        me = lax.axis_index(axis)
+        for step in range(1, size):
+            pl.semaphore_signal(
+                barrier, inc=1, device_id={axis: lax.rem(me + step, size)}, device_id_type=MESH
+            )
+    pl.semaphore_wait(barrier, n_tgt + n_sup - 2)
+
+    def bring(meanwhile):
+        if gathered:
+            gather_body(
+                n_tgt, channels, blocks, meanwhile, inputs[0], inputs[1], support[0], *gather_refs
+            )
+        else:
+            meanwhile()
+
+    tangent_body(
+        bring, n_sup, channels, support[0], *inputs[-3:], pred_ref, grad_ref, *tangent_refs
+    )
+    sizes, pieces, _ = all_reduce_scratch(grad_ref.shape[0], n_tgt)
+    all_reduce_body(sizes, pieces, False, grad_ref, out_ref, *refs)
 
 
 def local(n_tgt, n_sup, targets, labels, support_slots, block_owner, dual_coeffs):
-    blocks, per_block, _ = dual_coeffs.shape
+    blocks, per_block, classes = dual_coeffs.shape
     channels = targets.shape[1]
     pixels = targets.shape[2]
     supports = blocks * per_block
-    if supports == LANES and (pixels * per_block) % (n_tgt * LANES * 8) == 0:
-        s = gather(support_slots[0], block_owner, n_tgt)
+    vmem = pl.BlockSpec(memory_space=pltpu.VMEM)
+    smem = pl.BlockSpec(memory_space=pltpu.SMEM)
+    flat = pltpu.VMEM((channels * pixels, LANES), jnp.float32)
+    gathered = supports == LANES and (pixels * per_block) % (n_tgt * LANES * 8) == 0
+    if gathered:
+        x = pack_slot(support_slots[0], n_tgt)
+        first = (block_owner, x)
+        specs = [smem, vmem]
+        gather_refs = gather_scratch(x.shape, channels, n_tgt)
     else:
         mine = block_owner == lax.axis_index("tgt")
         slot = jnp.transpose(support_slots[0], (1, 2, 0))
         own = jnp.where(mine[None, None, :, None], slot[:, :, None, :], 0.0)
         own = own.reshape(channels * pixels, supports)
-        s = all_reduce(jnp.pad(own, ((0, 0), (0, LANES - supports))), n_tgt, 0)
-    s = s.reshape(channels, pixels, LANES)
-
-    predictions, grad = tangent(s, targets, labels, dual_coeffs, n_sup)
-    grad = all_reduce(grad.reshape(channels * pixels, LANES), n_tgt, 2)
+        first = (all_reduce(jnp.pad(own, ((0, 0), (0, LANES - supports))), n_tgt, 0),)
+        specs = [vmem]
+        gather_refs = []
+    field = pltpu.VMEM((SIDE + 2, SIDE + 2, 8, LANES), jnp.float32)
+    plain = pltpu.VMEM((SIDE, SIDE, 8, LANES), jnp.float32)
+    tangent_refs = [field] * 4 + [plain] * 6 + [
+        pltpu.VMEM((channels, SIDE, 8, LANES), jnp.float32),
+        pltpu.VMEM((3, SIDE, 8, LANES), jnp.float32),
+        pltpu.VMEM((channels, pixels, 1, LANES), jnp.float32),
+        pltpu.VMEM((3, pixels, 1, LANES), jnp.float32),
+        pltpu.VMEM((2, pixels + 2 * SIDE, LANES), jnp.float32),
+        pltpu.VMEM((6, pixels, LANES), jnp.float32),
+        pltpu.VMEM((channels, pixels, LANES), jnp.float32),
+        pltpu.VMEM((8, classes), jnp.float32),
+        pltpu.VMEM((n_sup - 1, 8, classes), jnp.float32),
+        pltpu.SemaphoreType.DMA((n_sup - 1,)),
+        pltpu.SemaphoreType.DMA((n_sup - 1,)),
+    ]
+    sum_refs = all_reduce_scratch(channels * pixels, n_tgt)[2]
+    predictions, grad = pl.pallas_call(
+        functools.partial(
+            program_body, n_tgt, n_sup, channels, blocks, gathered,
+            (len(gather_refs), len(tangent_refs)),
+        ),
+        out_shape=(
+            jax.ShapeDtypeStruct((8, classes), jnp.float32),
+            jax.ShapeDtypeStruct((channels * pixels, LANES), jnp.float32),
+        ),
+        in_specs=specs + [vmem, smem, vmem],
+        out_specs=(vmem, vmem),
+        scratch_shapes=[flat] * (1 + gathered) + gather_refs + tangent_refs + sum_refs,
+        compiler_params=pltpu.CompilerParams(
+            collective_id=1, has_side_effects=True, vmem_limit_bytes=62 << 20
+        ),
+        name="tangent_kernel",
+    )(*first, targets, labels, dual_coeffs)
     grad = grad.reshape(channels, pixels // LANES, LANES, LANES)[:, :, :supports]
     grad = jnp.transpose(grad, (2, 0, 1, 3)).reshape(blocks, per_block, channels, pixels)
     return predictions, grad

time: 137 us -> 130 us (0.949)
  Pallas kernels: 126 us -> 120 us
    pallas_call x3 -> x1, Pallas kernels: 126 us -> 120 us  [local(): pl.pallas_call(functools.partial(program_body, n_tgt, n_sup, channels, bl...]
    unnamed x12 -> x8, local copies, waits for them, and re-layouts: 7.46 us -> 4.03 us
    reshape x1, local copies, waits for them, and re-layouts: 0.92 us -> 2.32 us  [local(): grad.reshape(channels, pixels // LANES, LANES, LANES)[:, :, :supports]]
where the time goes in v1:
time: 130 us
  Pallas kernels  120 us (92%)
  local copies, waits for them, and re-layouts  8.7 us (7%)
    pallas_call x1, Pallas kernels, local(): pl.pallas_call(functools.partial(program_body, n_tgt, n_sup, channels, bl...  120 us
    unnamed x8, local copies, waits for them, and re-layouts  4.03 us

profile of v1, /device:TPU:0, one launch (start us, length us, event | category | flops | bytes accessed | tf_op | source)
XLA Modules:
  0.0 129.6 jit_solution(14074495632570303381)
XLA Ops:
  0.6 1.5 %copy.9 = f32[1,32,3,1024]{1,3,2,0:T(8,128)S(1)} copy(f32[1,32,3,1024]{3,1,2,0:T(8,128)} %param.7) | data formatting | bytes 786432 | tf_op args[2]
  2.1 0.7 copy.10
  2.8 0.0 copy-start
  2.8 1.4 %reshape.13.refs_1_ = f32[16,48,128]{2,1,0:T(8,128)} reshape(f32[16,3,16,4,32]{4,3,2,1,0:T(4,128)S(1)} %copy.10) | data formatting | bytes 786432 | tf_op jit(solution)/shard_map/reshape | solution.py:280
  4.2 0.0 copy-done
  4.2 0.7 copy.11.refs_2_
  5.0 120.2 %tangent_kernel.1 = (f32[8,100]{1,0:T(8,128)}, f32[3072,128]{1,0:T(8,128)}) custom-call(s32[4]{0:T(128)} %refs_0_.1, f32[16,48,128]{2,1,0:T(8,128)} %reshape.13.refs_1_, f32[8,3,1024]{2,1,0:T(4,128)} %copy.11.refs_2_, s32[8]{0:T(128)} %refs_3_.1, f32[4,32,100]{2,1,0:T(8,128)} %refs_4_.1), custom_call_target="tpu_custom_call" | custom-call | tf_op jit(solution)/shard_map/tangent_kernel/pallas_call | solution.py:697
  125.2 2.3 %copy.15 = f32[3,8,128,128]{3,1,2,0:T(8,128)S(1)} copy(f32[3,8,128,128]{3,2,1,0:T(8,128)} %bitcast.13) | data formatting | bytes 3145728 | tf_op jit(solution)/shard_map/reshape | solution.py:714
  127.5 0.2 reshape.15
  127.8 0.0 copy-start.1
  127.8 1.2 copy.13
  129.0 0.0 copy-done.1
  129.0 0.6 copy.17
Async XLA Ops:
  2.8 1.4 %copy-start = (f32[8,3,1024]{2,0,1:T(8,128)S(1)}, f32[8,3,1024]{2,0,1:T(8,128)}, u32[]{:S(2)}) copy-start(f32[8,3,1024]{2,0,1:T(8,128)} %param.5) | copy-start | bytes 294916
  127.8 1.3 copy-start.1
